TPU v7x, 256 devices: a whole 4x4x8 slice. The times are simulated.
256 devices in a mesh: ang: 64 (over x, z_hi, y, core), slab: 4 (over z_lo).
Axes of the slice: x: 4, y: 4, z: 8 (z_hi: 2, z_lo: 4; z = z_hi * 4 + z_lo), core: 2. Of those that a mesh axis runs over, the one named last changes fastest.
Arguments:
- volume: float32 [2, 512, 16384], P(None, ('ang', 'slab')), may hold values from -6 to 6
- tv_split: float32 [3, 2, 512, 16384], P(None, None, ('ang', 'slab')), may hold values from -6 to 6
- tv_dual: float32 [3, 2, 512, 16384], P(None, None, ('ang', 'slab')), may hold values from -4 to 4
- measured: float32 [128, 8, 2, 64, 8, 128], P('ang', None, None, None, 'slab'), may hold values from -6 to 6
- fit_dual: float32 [128, 8, 2, 64, 8, 128], P('ang', None, None, None, 'slab'), may hold values from -4 to 4
- footprints: bfloat16 [40, 128, 128], replicated, may hold values from -0.1875 to 0.1875
- voxel_tile: int32 [128, 8, 8], replicated, may hold values from 0 to 127
- kernel_pick: int32 [128, 8, 8], replicated, may hold values from 0 to 39
- tile_count: int32 [128, 8], replicated, may hold values from 4 to 8
Outputs:
- volume_next: float32 [2, 512, 16384], P(None, ('ang', 'slab'))
- split_next: float32 [3, 2, 512, 16384], P(None, None, ('ang', 'slab'))
- tv_dual_next: float32 [3, 2, 512, 16384], P(None, None, ('ang', 'slab'))
- fit_dual_next: float32 [128, 8, 2, 64, 8, 128], P('ang', None, None, None, 'slab')
Inputs may be any that keep to these rules, and one draw needn't show every extreme that they name: Only the first tile_count entries of a ray tile's list are live; tiles and kernels may repeat.
All inputs are finite; a program needn't handle non-finite values.
Results may differ from a plain program's by a relative error of at most 0.0068.
Values may be sent and summed in bfloat16 or wider, within the bound.
A program may use at most 128 MiB of HBM per device.

v0:
```python
import jax
import jax.numpy as jnp
from jax import lax
from jax.experimental import pallas as pl
from jax.experimental.pallas import tpu as pltpu
from jax.sharding import PartitionSpec as P

TILE_WIDTH = 128
VOLUME_CHANNELS = 2
KT = 128
NB = 40
NNZ = 8
RAYS = 8
PEERS = 32
ROWS = 16
PLANES = 4
ALL_ROWS = PEERS * ROWS
DEAD = NB * KT

penalty_tv = 0.5
tv_weight = 0.3
step_size = 0.3

F32 = jnp.float32
BF16 = jnp.bfloat16
MESH = pl.DeviceIdType.MESH


def kernel(
    codes, code_lanes, vol_hbm, split_hbm, tvd_hbm, meas_hbm, dual_hbm, foot_hbm,
    vol_out, split_out, tvd_out, fit_out,
    vol_v, split_v, tvd_v, meas_v, dual_v, foot_v,
    foot_wide, vol_send, vol_recv, vol_rows, vol_low, bank, counts, grouped,
    meas_send, meas_recv, proj_send, proj_recv, resid, ray_rows,
    first_send, first_recv, last_send, last_recv, part_send, part_recv, back_own, adj_v,
    next_send, next_recv,
    local_sem, out_sem, meas_ssem, meas_rsem, proj_ssem, proj_rsem, one_ssem, one_rsem,
):
    ang = lax.axis_index("ang")
    slab = lax.axis_index("slab")
    xi = ang // 16
    half = (ang // 8) % 2
    wi = ang % 8
    yi = wi // 2
    core = wi % 2
    me = xi * 8 + wi
    other = (xi * 16 + (1 - half) * 8 + wi, slab)
    pos = ang * 4 + slab
    up = (pos + 1) % 256
    down = (pos + 255) % 256
    up_id = (up // 4, up % 4)
    down_id = (down // 4, down % 4)
    keep = (pos < 255).astype(F32)
    keep_below = (pos > 0).astype(F32)

    def peer_of(i):
        px = (xi + i // 8) % 4
        py = (yi + (i // 2) % 4) % 4
        pc = (core + i % 2) % 2
        return px, py * 2 + pc

    local = [
        pltpu.make_async_copy(vol_hbm, vol_v, local_sem.at[0]),
        pltpu.make_async_copy(meas_hbm, meas_v, local_sem.at[1]),
        pltpu.make_async_copy(split_hbm, split_v, local_sem.at[2]),
        pltpu.make_async_copy(tvd_hbm, tvd_v, local_sem.at[3]),
        pltpu.make_async_copy(foot_hbm, foot_v, local_sem.at[4]),
        pltpu.make_async_copy(dual_hbm, dual_v, local_sem.at[5]),
    ]
    for copy in local:
        copy.start()

    barrier = pltpu.get_barrier_semaphore()

    @pl.loop(1, PEERS)
    def _(i):
        px, pw = peer_of(i)
        pl.semaphore_signal(
            barrier, inc=1, device_id=(px * 16 + half * 8 + pw, slab), device_id_type=MESH
        )

    for device in (other, up_id, down_id):
        pl.semaphore_signal(barrier, inc=1, device_id=device, device_id_type=MESH)

    def plane(ref, lead, z):
        return ref[pl.ds(lead * 256 + z, KT, stride=2), :]

    local[0].wait()
    for z in range(2):
        for c in range(2):
            cz = z * 2 + c
            image = plane(vol_v, c, z)
            vol_rows[pl.ds(cz, KT, stride=8), :] = image
            vol_send[cz] = image.astype(BF16)

    pl.semaphore_wait(barrier, PEERS + 2)

    def remote(src, dst, slot, device):
        return pltpu.make_async_remote_copy(
            src_ref=src, dst_ref=dst, send_sem=one_ssem.at[slot], recv_sem=one_rsem.at[slot],
            device_id=device, device_id_type=MESH,
        )

    vol_copy = remote(vol_send, vol_recv, 0, other)
    vol_copy.start()
    first_copy = remote(vol_send.at[pl.ds(0, 2)], first_recv, 1, down_id)
    first_copy.start()

    local[1].wait()

    def slice_row(px, pw, part, z, c):
        zh = px * 16 + ((half + part) % 2) * 8 + pw
        return c * 128 + zh * 2 + z

    def message(px, pw):
        peer = px * 8 + pw
        for part in range(2):
            for z in range(2):
                for c in range(2):
                    start = slice_row(px, pw, part, z, c)
                    rows = meas_v[pl.ds(start, ROWS, stride=256), :]
                    meas_send[peer, part * 4 + z * 2 + c] = rows.astype(BF16)

    def exchange(send, recv, ssem, rsem, px, pw):
        return pltpu.make_async_remote_copy(
            src_ref=send.at[px * 8 + pw], dst_ref=recv.at[me],
            send_sem=ssem.at[px * 8 + pw], recv_sem=rsem.at[me],
            device_id=(px * 16 + half * 8 + pw, slab), device_id_type=MESH,
        )

    def arrival(send, recv, ssem, rsem, px, pw):
        return pltpu.make_async_remote_copy(
            src_ref=send.at[px * 8 + pw], dst_ref=recv.at[px * 8 + pw],
            send_sem=ssem.at[px * 8 + pw], recv_sem=rsem.at[px * 8 + pw],
            device_id=(px * 16 + half * 8 + pw, slab), device_id_type=MESH,
        )

    @pl.loop(1, PEERS)
    def _(i):
        px, pw = peer_of(i)
        message(px, pw)
        exchange(meas_send, meas_recv, meas_ssem, meas_rsem, px, pw).start()

    message(xi, wi)
    for cz in range(8):
        meas_recv[me, cz] = meas_send[me, cz]

    local[2].wait()
    local[3].wait()
    for c in range(2):
        term = plane(tvd_v, c, 1) / penalty_tv - plane(split_v, c, 1) - plane(vol_v, c, 1)
        last_send[c] = term.astype(BF16)
    last_copy = remote(last_send, last_recv, 2, up_id)
    last_copy.start()

    @pl.loop(0, 32)
    def _(step):
        kc = step // 4
        lt = step % 4
        lanes = pl.ds(pl.multiple_of(lt * 128, 128), 128)
        tile = lax.broadcasted_iota(jnp.int32, (16, 128), 0) + kc * 16
        picks = []
        for j in range(NNZ):
            code = jnp.broadcast_to(code_lanes[j:j + 1, lanes], (16, 128))
            pick = jnp.where((code % 128) == tile, code // 128, -1)
            picks.append(pick.astype(F32).astype(BF16))
        one = jnp.ones((16, 128), BF16)
        zero = jnp.zeros((16, 128), BF16)
        for b in range(NB):
            hits = [jnp.where(pick == jnp.asarray(b, BF16), one, zero) for pick in picks]
            while len(hits) > 1:
                hits = [hits[n] + hits[n + 1] for n in range(0, len(hits), 2)]
            counts[pl.ds(pl.multiple_of(b * 128 + kc * 16, 16), 16), lanes] = hits[0]

    local[4].wait()
    for b in range(NB):
        foot_wide[:, b * 128:(b + 1) * 128] = foot_v[b]

    vol_copy.wait_recv()
    for cz in range(PLANES):
        vol_rows[pl.ds(4 + cz, KT, stride=8), :] = vol_recv[cz].astype(F32)
    vol_low[...] = vol_rows[...].astype(BF16)

    @pl.loop(0, NB // 2)
    def _(step):
        cols = pl.ds(pl.multiple_of(step * 256, 256), 256)
        for part in range(4):
            out = jnp.dot(
                vol_low[part * 256:(part + 1) * 256, :], foot_wide[:, cols],
                preferred_element_type=F32,
            )
            for n in range(2):
                bank[pl.ds((step * 2 + n) * 128 + part * 32, 32)] = (
                    out[:, n * 128:(n + 1) * 128].reshape(32, 8, 128)
                )

    bank[DEAD] = jnp.zeros((8, 128), F32)

    def project(px, pw):
        peer = px * 8 + pw
        for row in range(ROWS):
            at = peer * (ROWS * NNZ) + row * NNZ
            got = [bank[codes[at + j]] for j in range(NNZ)]
            while len(got) > 1:
                got = [got[n] + got[n + 1] for n in range(0, len(got), 2)]
            ray_rows[row * 8:(row + 1) * 8, :] = got[0]
        for cz in range(8):
            proj_send[peer, cz] = ray_rows[pl.ds(cz, ROWS, stride=8), :].astype(BF16)

    @pl.loop(1, PEERS)
    def _(i):
        px, pw = peer_of(i)
        project(px, pw)
        exchange(proj_send, proj_recv, proj_ssem, proj_rsem, px, pw).start()

    project(xi, wi)
    for cz in range(8):
        proj_recv[me, cz] = proj_send[me, cz]

    def subtract(px, pw):
        peer = px * 8 + pw
        rows = pl.ds(pl.multiple_of(peer * ROWS, ROWS), ROWS)
        for cz in range(8):
            gap = proj_send[peer, cz].astype(F32) - meas_recv[peer, cz].astype(F32)
            resid[cz // 4, rows, (cz % 4) * 128:(cz % 4 + 1) * 128] = gap.astype(BF16)

    subtract(xi, wi)

    @pl.loop(1, PEERS)
    def _(i):
        px, pw = peer_of(i)
        arrival(meas_send, meas_recv, meas_ssem, meas_rsem, px, pw).wait_recv()
        subtract(px, pw)

    def backward(part):
        @pl.loop(0, NB // 2)
        def _(step):
            rows = pl.ds(pl.multiple_of(step * 256, 256), 256)
            out = jnp.dot(counts[rows, :], resid[part], preferred_element_type=F32).astype(BF16)
            for n in range(2):
                cols = pl.ds(pl.multiple_of((step * 2 + n) * 128, 128), 128)
                for cz in range(PLANES):
                    grouped[cz * 128:(cz + 1) * 128, cols] = (
                        out[n * 128:(n + 1) * 128, cz * 128:(cz + 1) * 128]
                    )
        return lax.dot_general(
            grouped[...], foot_wide[...], (((1,), (1,)), ((), ())), preferred_element_type=F32
        )

    theirs = backward(1)
    for cz in range(PLANES):
        part_send[cz] = theirs[cz * 128:(cz + 1) * 128, :].astype(BF16)
    part_copy = remote(part_send, part_recv, 3, other)
    part_copy.start()
    back_own[...] = backward(0)

    row_at = lax.broadcasted_iota(jnp.int32, (KT, TILE_WIDTH), 0)
    col_at = lax.broadcasted_iota(jnp.int32, (KT, TILE_WIDTH), 1)
    inner_row = row_at < KT - 1
    inner_col = col_at < TILE_WIDTH - 1

    def along(image, axis):
        step = pltpu.roll(image, 127, axis) - image
        return jnp.where(inner_row if axis == 0 else inner_col, step, 0.0)

    def spread(part, axis):
        part = jnp.where(inner_row if axis == 0 else inner_col, part, 0.0)
        return pltpu.roll(part, 1, axis) - part

    def force(i, c, z):
        return plane(tvd_v, i * 2 + c, z) / penalty_tv - plane(split_v, i * 2 + c, z)

    first_copy.wait_recv()
    last_copy.wait_recv()
    for c in range(2):
        images = [plane(vol_v, c, z) for z in range(2)]
        below = (last_recv[c].astype(F32) + images[0]) * keep_below
        middle = images[1] - images[0] + force(0, c, 0)
        above = (first_recv[c].astype(F32) - images[1] + force(0, c, 1)) * keep
        for z, slices in enumerate((below - middle, middle - above)):
            total = slices
            for axis in range(2):
                total = total + spread(along(images[z], axis) + force(1 + axis, c, z), axis)
            adj_v[z * 2 + c] = penalty_tv * total

    part_copy.wait_recv()
    for z in range(2):
        for c in range(2):
            cz = z * 2 + c
            descent = back_own[cz * 128:(cz + 1) * 128, :] + part_recv[cz].astype(F32) + adj_v[cz]
            image = plane(vol_v, c, z) - step_size * descent
            vol_v[pl.ds(c * 256 + z, KT, stride=2), :] = image
            if z == 0:
                next_send[c] = image.astype(BF16)
        if z == 0:
            next_copy = remote(next_send, next_recv, 4, down_id)
            next_copy.start()
    vol_done = pltpu.make_async_copy(vol_v, vol_out, out_sem.at[0])
    vol_done.start()

    local[5].wait()

    def fit(px, pw):
        peer = px * 8 + pw
        for part in range(2):
            for z in range(2):
                for c in range(2):
                    rows = pl.ds(slice_row(px, pw, part, z, c), ROWS, stride=256)
                    proj = proj_recv[peer, part * 4 + z * 2 + c].astype(F32)
                    dual_v[rows, :] = 0.5 * (proj + dual_v[rows, :] - meas_v[rows, :])

    fit(xi, wi)

    @pl.loop(1, PEERS)
    def _(i):
        px, pw = peer_of(i)
        arrival(proj_send, proj_recv, proj_ssem, proj_rsem, px, pw).wait_recv()
        fit(px, pw)

    fit_done = pltpu.make_async_copy(dual_v, fit_out, out_sem.at[1])
    fit_done.start()

    next_copy.wait_recv()
    for c in range(2):
        images = [plane(vol_v, c, z) for z in range(2)]
        above = (next_recv[c].astype(F32) - images[1]) * keep
        for z, slices in enumerate((images[1] - images[0], above)):
            steps = (slices, along(images[z], 0), along(images[z], 1))
            for i in range(3):
                rows = pl.ds((i * 2 + c) * 256 + z, KT, stride=2)
                dual = tvd_v[rows, :]
                arg = steps[i] + dual / penalty_tv
                bound = tv_weight / penalty_tv
                split = arg - jnp.clip(arg, -bound, bound)
                split_v[rows, :] = split
                tvd_v[rows, :] = dual + penalty_tv * (steps[i] - split)
    split_done = pltpu.make_async_copy(split_v, split_out, out_sem.at[2])
    split_done.start()
    tvd_done = pltpu.make_async_copy(tvd_v, tvd_out, out_sem.at[3])
    tvd_done.start()

    for copy in (vol_copy, first_copy, last_copy, part_copy, next_copy):
        copy.wait_send()

    @pl.loop(1, PEERS)
    def _(i):
        px, pw = peer_of(i)
        exchange(meas_send, meas_recv, meas_ssem, meas_rsem, px, pw).wait_send()
        exchange(proj_send, proj_recv, proj_ssem, proj_rsem, px, pw).wait_send()

    for copy in (vol_done, fit_done, split_done, tvd_done):
        copy.wait()


def to_rows(array):
    lead = array.shape[:-2]
    tiles = array.reshape(*lead, 2, KT, TILE_WIDTH)
    return jnp.swapaxes(tiles, -3, -2).reshape(-1, TILE_WIDTH)


def from_rows(rows, shape):
    tiles = rows.reshape(*shape[:-2], KT, 2, TILE_WIDTH)
    return jnp.swapaxes(tiles, -3, -2).reshape(shape)


def shards(
    volume, tv_split, tv_dual, measured, fit_dual, footprints, voxel_tile, kernel_pick, tile_count
):
    half = (lax.axis_index("ang") // 8) % 2
    code = kernel_pick * KT + voxel_tile
    live = jnp.arange(NNZ, dtype=jnp.int32) < tile_count[:, :, None]
    code = jnp.where(live, code, DEAD).reshape(4, 2, 16, RAYS, NNZ)
    code = lax.dynamic_index_in_dim(code, half, 1, keepdims=False).reshape(ALL_ROWS, NNZ)

    hbm = pl.BlockSpec(memory_space=pl.ANY)
    vmem = pl.BlockSpec(memory_space=pltpu.VMEM)
    tile = (KT, TILE_WIDTH)
    volume_next, split_next, tv_dual_next, fit_dual_next = pl.pallas_call(
        kernel,
        out_shape=[
            jax.ShapeDtypeStruct((512, 128), F32),
            jax.ShapeDtypeStruct((1536, 128), F32),
            jax.ShapeDtypeStruct((1536, 128), F32),
            jax.ShapeDtypeStruct((4096, 128), F32),
        ],
        in_specs=[pl.BlockSpec(memory_space=pltpu.SMEM), vmem] + [hbm] * 6,
        out_specs=[hbm] * 4,
        scratch_shapes=[
            pltpu.VMEM((512, 128), F32),
            pltpu.VMEM((1536, 128), F32),
            pltpu.VMEM((1536, 128), F32),
            pltpu.VMEM((4096, 128), F32),
            pltpu.VMEM((4096, 128), F32),
            pltpu.VMEM((NB, 128, 128), BF16),
            pltpu.VMEM((128, NB * 128), BF16),
            pltpu.VMEM((PLANES, *tile), BF16),
            pltpu.VMEM((PLANES, *tile), BF16),
            pltpu.VMEM((1024, 128), F32),
            pltpu.VMEM((1024, 128), BF16),
            pltpu.VMEM((NB * KT + 8, 8, 128), F32),
            pltpu.VMEM((NB * KT, ALL_ROWS), BF16),
            pltpu.VMEM((512, NB * 128), BF16),
            pltpu.VMEM((PEERS, 8, ROWS, 128), BF16),
            pltpu.VMEM((PEERS, 8, ROWS, 128), BF16),
            pltpu.VMEM((PEERS, 8, ROWS, 128), BF16),
            pltpu.VMEM((PEERS, 8, ROWS, 128), BF16),
            pltpu.VMEM((2, ALL_ROWS, 512), BF16),
            pltpu.VMEM((ROWS * 8, 128), F32),
            pltpu.VMEM((2, *tile), BF16),
            pltpu.VMEM((2, *tile), BF16),
            pltpu.VMEM((2, *tile), BF16),
            pltpu.VMEM((2, *tile), BF16),
            pltpu.VMEM((PLANES, *tile), BF16),
            pltpu.VMEM((PLANES, *tile), BF16),
            pltpu.VMEM((512, 128), F32),
            pltpu.VMEM((PLANES, *tile), F32),
            pltpu.VMEM((2, *tile), BF16),
            pltpu.VMEM((2, *tile), BF16),
            pltpu.SemaphoreType.DMA((6,)),
            pltpu.SemaphoreType.DMA((4,)),
            pltpu.SemaphoreType.DMA((PEERS,)),
            pltpu.SemaphoreType.DMA((PEERS,)),
            pltpu.SemaphoreType.DMA((PEERS,)),
            pltpu.SemaphoreType.DMA((PEERS,)),
            pltpu.SemaphoreType.DMA((5,)),
            pltpu.SemaphoreType.DMA((5,)),
        ],
        compiler_params=pltpu.CompilerParams(
            collective_id=0, has_side_effects=True, vmem_limit_bytes=60 * 1024 * 1024
        ),
    )(
        code.reshape(-1), code.T,
        to_rows(volume), to_rows(tv_split), to_rows(tv_dual),
        measured.reshape(4096, 128), fit_dual.reshape(4096, 128), footprints,
    )
    return (
        from_rows(volume_next, volume.shape),
        from_rows(split_next, tv_split.shape),
        from_rows(tv_dual_next, tv_dual.shape),
        fit_dual_next.reshape(fit_dual.shape),
    )


def solution(mesh):
    return jax.shard_map(
        shards,
        mesh=mesh,
        in_specs=(
            P(None, ("ang", "slab"), None),
            P(None, None, ("ang", "slab"), None),
            P(None, None, ("ang", "slab"), None),
            P("ang", None, None, None, "slab", None),
            P("ang", None, None, None, "slab", None),
            P(),
            P(),
            P(),
            P(),
        ),
        out_specs=(
            P(None, ("ang", "slab"), None),
            P(None, None, ("ang", "slab"), None),
            P(None, None, ("ang", "slab"), None),
            P("ang", None, None, None, "slab", None),
        ),
        check_vma=False,
    )
```

profile of v0, /device:TPU:1, one launch (start us, length us, event | category | flops | bytes accessed | tf_op | source)
XLA Modules:
  0.0 68.7 jit_solution(4053268817318500648)
XLA Ops:
  0.7 0.8 %add_select_fusion = s32[128,8,8]{0,2,1:T(8,128)S(1)} fusion(s32[128,8,8]{0,2,1:T(8,128)} %param.15, s32[128,8,8]{0,2,1:T(8,128)} %param.16, s32[128,8]{0,1:T(8,128)} %param.17), kind=kLoop, calls=%fused_computation | loop fusion | flops 32768 | bytes 102400 | tf_op jit(solution)/shard_map/jit(_where)/select_n | solution.py:372
  1.5 0.4 reshape.62
  1.8 0.1 constant_dynamic-slice_fusion
  2.0 0.2 copy.21
  2.1 0.8 %reshape_reshape.3.codes = s32[4096]{0:T(1024)} reshape(s32[4,1,16,8,8]{4,3,2,0,1:T(8,128)S(1)} %copy.21) | data formatting | bytes 32768 | tf_op jit(solution)/shard_map/reshape;reshape | solution.py:432
  2.9 0.1 copy.28
  3.0 0.8 %reshape.63 = s32[512,8]{0,1:T(8,128)} reshape(s32[4,1,16,8,8]{3,2,0,4,1:T(8,128)S(1)} %copy.28) | data formatting | bytes 32768 | tf_op jit(solution)/shard_map/reshape | solution.py:373
  3.8 57.6 %shard_map.120 = (f32[512,128]{1,0:T(8,128)}, f32[1536,128]{1,0:T(8,128)}, f32[1536,128]{1,0:T(8,128)}, f32[4096,128]{1,0:T(8,128)}) custom-call(s32[4096]{0:T(1024)} %reshape_reshape.3.codes, s32[8,512]{1,0:T(8,128)} %bitcast.53, f32[512,128]{1,0:T(8,128)} %bitcast.51, f32[1536,128]{1,0:T(8,128)} %bitcast.47, f32[1536,128]{1,0:T(8,128)} %bitcast.48, ...), custom_call_target="tpu_custom_call" | custom-call | tf_op jit(solution)/shard_map/pallas_call | solution.py:378
  61.4 0.0 copy-start
  61.4 1.8 %copy.34 = f32[2,2,16384]{2,1,0:T(2,128)} copy(f32[2,2,16384]{2,1,0:T(2,128)} %bitcast.52) | data formatting | bytes 524288
  63.2 2.1 %copy.35 = f32[3,2,2,16384]{3,2,1,0:T(2,128)} copy(f32[3,2,2,16384]{3,2,1,0:T(2,128)} %bitcast.50) | data formatting | bytes 1572864
  65.3 2.1 %copy.36 = f32[3,2,2,16384]{3,2,1,0:T(2,128)} copy(f32[3,2,2,16384]{3,2,1,0:T(2,128)} %bitcast.49) | data formatting | bytes 1572864
  67.3 0.0 copy-done
  67.3 1.3 %copy.37 = f32[2,8,2,64,2,128]{5,4,3,2,1,0:T(2,128)} copy(f32[2,8,2,64,2,128]{5,4,3,2,1,0:T(2,128)S(1)} %bitcast.46) | data formatting | bytes 4194304
Async XLA Ops:
  61.4 6.0 %copy-start = (f32[4096,128]{1,0:T(8,128)S(1)}, f32[4096,128]{1,0:T(8,128)}, u32[]{:S(2)}) copy-start(f32[4096,128]{1,0:T(8,128)} %get-tuple-element.11) | copy-start | bytes 6291460
where the time goes:
time: 69 us; the launch traced here: 68.7 us
  Pallas kernels  57.6 us (83%)
  local copies, waits for them, and re-layouts  9.59 us (14%)
  other arithmetic  0.78 us (1%)
  between operations  0.72 us (1%)
    pallas_call x1, Pallas kernels, shards(): pl.pallas_call(kernel, out_shape=[jax.ShapeDtypeStruct((512, 128), F32),...  57.6 us
    unnamed x7, local copies, waits for them, and re-layouts  7.41 us

commit v1 on v0

v1 whole, which is shorter than its diff:
```python
import jax
import jax.numpy as jnp
from jax import lax
from jax.experimental import pallas as pl
from jax.experimental.pallas import tpu as pltpu
from jax.sharding import PartitionSpec as P

TILE_WIDTH = 128
VOLUME_CHANNELS = 2
KT = 128
NB = 40
NNZ = 8
RAYS = 8
PEERS = 32
ROWS = 16
PLANES = 4
ALL_ROWS = PEERS * ROWS
DEAD = NB * KT
RUNS = 4
RUN = KT // RUNS
TALL = 8

penalty_tv = 0.5
tv_weight = 0.3
step_size = 0.3

F32 = jnp.float32
BF16 = jnp.bfloat16
MESH = pl.DeviceIdType.MESH


def kernel(
    tile_ref, pick_ref, live_ref, vol_hbm, split_hbm, tvd_hbm, meas_hbm, dual_hbm, foot_hbm,
    vol_out, split_out, tvd_out, fit_out,
    vol_v, split_v, tvd_v, meas_v, dual_v, foot_v,
    foot_wide, vol_send, vol_recv, vol_rows, bank, counts, grouped,
    meas_send, meas_recv, proj_send, proj_recv, resid, ray_rows,
    first_recv, last_send, last_recv, part_send, part_recv, back_own, adj_v,
    next_send, next_recv, code_v, codes, lanes_v,
    local_sem, out_sem, meas_ssem, meas_rsem, proj_ssem, proj_rsem, one_ssem, one_rsem,
):
    ang = lax.axis_index("ang")
    slab = lax.axis_index("slab")
    xi = ang // 16
    half = (ang // 8) % 2
    wi = ang % 8
    yi = wi // 2
    core = wi % 2
    me = xi * 8 + wi
    other = (xi * 16 + (1 - half) * 8 + wi, slab)
    pos = ang * 4 + slab
    up = (pos + 1) % 256
    down = (pos + 255) % 256
    up_id = (up // 4, up % 4)
    down_id = (down // 4, down % 4)
    keep = (pos < 255).astype(F32)
    keep_below = (pos > 0).astype(F32)

    def peer_of(i):
        n = i % 16
        px = (xi + 4 - n % 4) % 4
        py = (yi + 8 - n % 4 - n // 4) % 4
        pc = (core + i // 16) % 2
        return px, py * 2 + pc

    def far_peer(i):
        px = (xi + 6 - i // 8) % 4
        py = (yi + 6 - i // 2 % 4) % 4
        return px, py * 2 + i % 2

    def ang_of(px, pw):
        return px * 16 + half * 8 + pw

    local = [
        pltpu.make_async_copy(vol_hbm, vol_v, local_sem.at[0]),
        pltpu.make_async_copy(meas_hbm, meas_v, local_sem.at[1]),
        pltpu.make_async_copy(split_hbm, split_v, local_sem.at[2]),
        pltpu.make_async_copy(tvd_hbm, tvd_v, local_sem.at[3]),
        pltpu.make_async_copy(foot_hbm, foot_v, local_sem.at[4]),
        pltpu.make_async_copy(dual_hbm, dual_v, local_sem.at[5]),
    ]
    for copy in local:
        copy.start()

    barrier = pltpu.get_barrier_semaphore()

    pl.semaphore_signal(barrier, inc=1, device_id=other, device_id_type=MESH)

    @pl.loop(0, PEERS)
    def _(i):
        px, pw = far_peer(i)

        @pl.when(px * 8 + pw != me)
        def _():
            pl.semaphore_signal(
                barrier, inc=1, device_id=(ang_of(px, pw), slab), device_id_type=MESH
            )

    for device in (up_id, down_id):
        pl.semaphore_signal(barrier, inc=1, device_id=device, device_id_type=MESH)

    def plane(ref, lead, z):
        return ref[pl.ds(lead * 256 + z, KT, stride=2), :]

    local[0].wait()
    for z in range(2):
        for c in range(2):
            cz = z * 2 + c
            image = plane(vol_v, c, z)
            vol_rows[pl.ds(c * 2 + z, KT, stride=8), :] = image
            for run in range(RUNS):
                vol_send[run, cz] = image[run * RUN:(run + 1) * RUN, :].astype(BF16)

    local[1].wait()

    def slice_row(px, pw, part, z, c):
        zh = px * 16 + ((half + part) % 2) * 8 + pw
        return c * 128 + zh * 2 + z

    def message(px, pw):
        peer = px * 8 + pw
        for part in range(2):
            for z in range(2):
                for c in range(2):
                    start = slice_row(px, pw, part, z, c)
                    rows = meas_v[pl.ds(start, ROWS, stride=256), :]
                    meas_send[peer, part * 4 + z * 2 + c] = rows.astype(BF16)

    @pl.loop(0, PEERS)
    def _(peer):
        message(peer // 8, peer % 8)

    for cz in range(8):
        meas_recv[me, cz] = meas_send[me, cz]

    def exchange(send, recv, ssem, rsem, px, pw):
        return pltpu.make_async_remote_copy(
            src_ref=send.at[px * 8 + pw], dst_ref=recv.at[me],
            send_sem=ssem.at[px * 8 + pw], recv_sem=rsem.at[me],
            device_id=(ang_of(px, pw), slab), device_id_type=MESH,
        )

    def arrival(send, recv, ssem, rsem, px, pw):
        return pltpu.make_async_remote_copy(
            src_ref=send.at[px * 8 + pw], dst_ref=recv.at[px * 8 + pw],
            send_sem=ssem.at[px * 8 + pw], recv_sem=rsem.at[px * 8 + pw],
            device_id=(ang_of(px, pw), slab), device_id_type=MESH,
        )

    pl.semaphore_wait(barrier, PEERS + 2)

    def remote(src, dst, slot, device):
        return pltpu.make_async_remote_copy(
            src_ref=src, dst_ref=dst, send_sem=one_ssem.at[slot], recv_sem=one_rsem.at[slot],
            device_id=device, device_id_type=MESH,
        )

    vol_copies = [
        remote(vol_send.at[run], vol_recv.at[run], run, other) for run in range(RUNS)
    ]
    for copy in vol_copies:
        copy.start()

    @pl.loop(1, PEERS)
    def _(i):
        px, pw = peer_of(i)
        exchange(meas_send, meas_recv, meas_ssem, meas_rsem, px, pw).start()

    entry_at = lax.broadcasted_iota(jnp.int32, (NNZ, 128), 0)
    lane = lax.broadcasted_iota(jnp.int32, (128, ALL_ROWS), 1)
    angle_at = lax.broadcasted_iota(jnp.int32, (128, ALL_ROWS), 0)
    peer_at = lane // ROWS
    wanted = peer_at // 8 * 32 + half * 16 + peer_at % 8 * 2 + lane // RAYS % 2
    same_angle = wanted == angle_at
    found = jnp.zeros((2 * NNZ, ALL_ROWS), F32)
    for r in range(RAYS):
        rows = slice(r * NNZ, (r + 1) * NNZ)
        is_live = entry_at < live_ref[r:r + 1, :]
        tiles = tile_ref[rows, :]
        picks = jnp.where(is_live, pick_ref[rows, :], NB)
        code_v[rows, :] = jnp.where(is_live, picks * KT + tiles, DEAD)
        both = jnp.concatenate([tiles, picks], axis=0).astype(F32).astype(BF16)
        chosen = jnp.where(same_angle & (lane % RAYS == r), 1.0, 0.0).astype(BF16)
        found = found + jnp.dot(both, chosen, preferred_element_type=F32)
    lanes_v[...] = found
    codes_copy = pltpu.make_async_copy(code_v, codes, local_sem.at[6])
    codes_copy.start()

    local[4].wait()
    for b in range(NB):
        foot_wide[:, b * 128:(b + 1) * 128] = foot_v[b]

    @pl.loop(0, 32)
    def _(step):
        kc = step // 4
        lt = step % 4
        lanes = pl.ds(pl.multiple_of(lt * 128, 128), 128)
        tile = (lax.broadcasted_iota(jnp.int32, (16, 128), 0) + kc * 16).astype(F32)
        picks = []
        for j in range(NNZ):
            held = jnp.broadcast_to(lanes_v[j:j + 1, lanes], (16, 128)) == tile
            pick = jnp.broadcast_to(lanes_v[NNZ + j:NNZ + j + 1, lanes], (16, 128))
            picks.append(jnp.where(held, pick, -1.0).astype(BF16))
        one = jnp.ones((16, 128), BF16)
        zero = jnp.zeros((16, 128), BF16)
        for b in range(NB):
            hits = [jnp.where(pick == jnp.asarray(b, BF16), one, zero) for pick in picks]
            while len(hits) > 1:
                hits = [hits[n] + hits[n + 1] for n in range(0, len(hits), 2)]
            counts[pl.ds(pl.multiple_of(b * 128 + kc * 16, 16), 16), lanes] = hits[0]

    for run in range(RUNS):
        vol_copies[run].wait_recv()
        for z in range(2):
            for c in range(2):
                at = pl.ds(run * RUN * 8 + 4 + c * 2 + z, RUN, stride=8)
                vol_rows[at, :] = vol_recv[run, z * 2 + c].astype(F32)
        vol_low = vol_rows[run * RUN * 8:(run + 1) * RUN * 8, :].astype(BF16)

        @pl.loop(0, NB // 8)
        def _(step, run=run, vol_low=vol_low):
            cols = pl.ds(pl.multiple_of(step * 1024, 1024), 1024)
            out = jnp.dot(vol_low, foot_wide[:, cols], preferred_element_type=F32)
            for n in range(8):
                bank[pl.ds((step * 8 + n) * KT + run * RUN, RUN)] = (
                    out[:, n * 128:(n + 1) * 128].reshape(RUN, 8, 128)
                )

    first_copy = remote(vol_send.at[:, pl.ds(0, 2)], first_recv, RUNS, down_id)
    first_copy.start()

    local[2].wait()
    local[3].wait()
    for c in range(2):
        term = plane(tvd_v, c, 1) / penalty_tv - plane(split_v, c, 1) - plane(vol_v, c, 1)
        last_send[c] = term.astype(BF16)
    last_copy = remote(last_send, last_recv, RUNS + 1, up_id)
    last_copy.start()

    bank[DEAD] = jnp.zeros((8, 128), F32)

    codes_copy.wait()

    def project(px, pw):
        peer = px * 8 + pw
        for row in range(ROWS):
            angle = px * 32 + half * 16 + pw * 2 + row // RAYS
            got = [bank[codes[row % RAYS * NNZ + j, angle]] for j in range(NNZ)]
            while len(got) > 1:
                got = [got[n] + got[n + 1] for n in range(0, len(got), 2)]
            ray_rows[row * 8:(row + 1) * 8, :] = got[0]
        proj_send[peer] = ray_rows[...].astype(BF16)
        rows = pl.ds(pl.multiple_of(peer * ROWS, ROWS), ROWS)
        for part in range(2):
            for c in range(2):
                for z in range(2):
                    at = z * 2 + c
                    plane_rows = ray_rows[pl.ds(part * 4 + c * 2 + z, ROWS, stride=8), :]
                    resid[part, rows, at * 128:(at + 1) * 128] = plane_rows.astype(BF16)

    @pl.loop(1, PEERS)
    def _(i):
        px, pw = peer_of(i)
        project(px, pw)
        exchange(proj_send, proj_recv, proj_ssem, proj_rsem, px, pw).start()

    project(xi, wi)
    proj_recv[me] = proj_send[me]

    def subtract(px, pw):
        peer = px * 8 + pw
        rows = pl.ds(pl.multiple_of(peer * ROWS, ROWS), ROWS)
        for cz in range(8):
            cols = slice(cz % 4 * 128, (cz % 4 + 1) * 128)
            gap = resid[cz // 4, rows, cols].astype(F32) - meas_recv[peer, cz].astype(F32)
            resid[cz // 4, rows, cols] = gap.astype(BF16)

    subtract(xi, wi)

    @pl.loop(1, PEERS)
    def _(i):
        px, pw = peer_of(i)
        arrival(meas_send, meas_recv, meas_ssem, meas_rsem, px, pw).wait_recv()
        subtract(px, pw)

    def backward(part, planes):
        first, last = planes.start, planes.stop
        rows_at = (last - first) * 128

        @pl.loop(0, NB // TALL)
        def _(step):
            rows = pl.ds(pl.multiple_of(step * (TALL * KT), TALL * KT), TALL * KT)
            out = jnp.dot(
                counts[rows, :], resid[part, :, first * 128:last * 128],
                preferred_element_type=F32,
            ).astype(BF16)
            for n in range(TALL):
                cols = pl.ds(pl.multiple_of((step * TALL + n) * 128, 128), 128)
                for p in range(last - first):
                    grouped[p * 128:(p + 1) * 128, cols] = (
                        out[n * 128:(n + 1) * 128, p * 128:(p + 1) * 128]
                    )
        return lax.dot_general(
            grouped[:rows_at, :], foot_wide[...], (((1,), (1,)), ((), ())),
            preferred_element_type=F32,
        )

    part_copies = [
        remote(part_send.at[z], part_recv.at[z], RUNS + 2 + z, other) for z in range(2)
    ]
    for z in range(2):
        theirs = backward(1, slice(z * 2, z * 2 + 2))
        for c in range(2):
            part_send[z, c] = theirs[c * 128:(c + 1) * 128, :].astype(BF16)
        part_copies[z].start()
    back_own[...] = backward(0, slice(0, 4))

    row_at = lax.broadcasted_iota(jnp.int32, (KT, TILE_WIDTH), 0)
    col_at = lax.broadcasted_iota(jnp.int32, (KT, TILE_WIDTH), 1)
    inner_row = row_at < KT - 1
    inner_col = col_at < TILE_WIDTH - 1

    def along(image, axis):
        step = pltpu.roll(image, 127, axis) - image
        return jnp.where(inner_row if axis == 0 else inner_col, step, 0.0)

    def spread(part, axis):
        part = jnp.where(inner_row if axis == 0 else inner_col, part, 0.0)
        return pltpu.roll(part, 1, axis) - part

    def force(i, c, z):
        return plane(tvd_v, i * 2 + c, z) / penalty_tv - plane(split_v, i * 2 + c, z)

    first_copy.wait_recv()
    last_copy.wait_recv()
    for c in range(2):
        images = [plane(vol_v, c, z) for z in range(2)]
        below = (last_recv[c].astype(F32) + images[0]) * keep_below
        middle = images[1] - images[0] + force(0, c, 0)
        above = (first_recv[:, c].reshape(KT, 128).astype(F32) - images[1] + force(0, c, 1)) * keep
        for z, slices in enumerate((below - middle, middle - above)):
            total = slices
            for axis in range(2):
                total = total + spread(along(images[z], axis) + force(1 + axis, c, z), axis)
            adj_v[z * 2 + c] = penalty_tv * total

    for z in range(2):
        part_copies[z].wait_recv()
        for c in range(2):
            cz = z * 2 + c
            descent = back_own[cz * 128:(cz + 1) * 128, :] + part_recv[z, c].astype(F32) + adj_v[cz]
            image = plane(vol_v, c, z) - step_size * descent
            vol_v[pl.ds(c * 256 + z, KT, stride=2), :] = image
            if z == 0:
                next_send[c] = image.astype(BF16)
        if z == 0:
            next_copy = remote(next_send, next_recv, RUNS + 4, down_id)
            next_copy.start()
    vol_done = pltpu.make_async_copy(vol_v, vol_out, out_sem.at[0])
    vol_done.start()

    local[5].wait()

    @pl.loop(1, PEERS)
    def _(i):
        px, pw = peer_of(i)
        arrival(proj_send, proj_recv, proj_ssem, proj_rsem, px, pw).wait_recv()

    pair = lax.broadcasted_iota(jnp.int32, (8, 128), 0) // 2

    def one_of(pieces):
        low = jnp.where(pair == 0, pieces[0], pieces[1])
        high = jnp.where(pair == 2, pieces[2], pieces[3])
        return jnp.where(pair < 2, low, high)

    @pl.loop(0, PEERS // 4)
    def _(block):
        for two in range(ROWS // 2):
            wide = [
                proj_recv[block * 4 + n, two * 16:(two + 1) * 16, :].astype(F32) for n in range(4)
            ]
            for row in range(2):
                given = [tile[row * 8:(row + 1) * 8, :] for tile in wide]
                turned = [one_of([given[(g + d) % 4] for g in range(4)]) for d in range(4)]
                turned = [turned[0]] + [pltpu.roll(turned[d], 2 * d, 0) for d in range(1, 4)]
                for part in range(2):
                    for c in range(2):
                        g = part * 2 + c
                        proj = one_of([turned[(n - g) % 4] for n in range(4)])
                        at = (two * 2 + row) * 256 + c * 128 + block // 2 * 32 + block % 2 * 8
                        rows = pl.ds(pl.multiple_of(at + (half + part) % 2 * 16, 8), 8)
                        dual_v[rows, :] = 0.5 * (proj + dual_v[rows, :] - meas_v[rows, :])

    fit_done = pltpu.make_async_copy(dual_v, fit_out, out_sem.at[1])
    fit_done.start()

    for z in range(2):
        if z == 1:
            next_copy.wait_recv()
        for c in range(2):
            image = plane(vol_v, c, z)
            if z == 0:
                slices = plane(vol_v, c, 1) - image
            else:
                slices = (next_recv[c].astype(F32) - image) * keep
            steps = (slices, along(image, 0), along(image, 1))
            for i in range(3):
                rows = pl.ds((i * 2 + c) * 256 + z, KT, stride=2)
                dual = tvd_v[rows, :]
                arg = steps[i] + dual / penalty_tv
                bound = tv_weight / penalty_tv
                split = arg - jnp.clip(arg, -bound, bound)
                split_v[rows, :] = split
                tvd_v[rows, :] = dual + penalty_tv * (steps[i] - split)
    split_done = pltpu.make_async_copy(split_v, split_out, out_sem.at[2])
    split_done.start()
    tvd_done = pltpu.make_async_copy(tvd_v, tvd_out, out_sem.at[3])
    tvd_done.start()

    for copy in (*vol_copies, first_copy, last_copy, *part_copies, next_copy):
        copy.wait_send()

    @pl.loop(1, PEERS)
    def _(i):
        px, pw = peer_of(i)
        exchange(meas_send, meas_recv, meas_ssem, meas_rsem, px, pw).wait_send()
        exchange(proj_send, proj_recv, proj_ssem, proj_rsem, px, pw).wait_send()

    for copy in (vol_done, fit_done, split_done, tvd_done):
        copy.wait()


def hand_on(*refs):
    given, out, held = refs[:4], refs[4:8], refs[8:12]
    sems = refs[12]
    fetches = [pltpu.make_async_copy(given[n], held[n], sems.at[n]) for n in range(4)]
    stores = [pltpu.make_async_copy(held[n], out[n], sems.at[4 + n]) for n in range(4)]
    for copy in fetches:
        copy.start()
    for fetch, store in zip(fetches, stores):
        fetch.wait()
        store.start()
    for copy in stores:
        copy.wait()


def to_rows(array):
    lead = array.shape[:-2]
    tiles = array.reshape(*lead, 2, KT, TILE_WIDTH)
    return jnp.swapaxes(tiles, -3, -2).reshape(-1, TILE_WIDTH)


def from_rows(rows, shape):
    tiles = rows.reshape(*shape[:-2], KT, 2, TILE_WIDTH)
    return jnp.swapaxes(tiles, -3, -2).reshape(shape)


def shards(
    volume, tv_split, tv_dual, measured, fit_dual, footprints, voxel_tile, kernel_pick, tile_count
):
    lists = [array.transpose(1, 2, 0).reshape(-1, 128) for array in (voxel_tile, kernel_pick)]

    hbm = pl.BlockSpec(memory_space=pl.ANY)
    vmem = pl.BlockSpec(memory_space=pltpu.VMEM)
    tile = (KT, TILE_WIDTH)
    result = [
        jax.ShapeDtypeStruct((512, 128), F32),
        jax.ShapeDtypeStruct((1536, 128), F32),
        jax.ShapeDtypeStruct((1536, 128), F32),
        jax.ShapeDtypeStruct((4096, 128), F32),
    ]
    held = pl.pallas_call(
        kernel,
        out_shape=result,
        in_specs=[vmem] * 3 + [hbm] * 6,
        out_specs=[hbm] * 4,
        scratch_shapes=[
            pltpu.VMEM((512, 128), F32),
            pltpu.VMEM((1536, 128), F32),
            pltpu.VMEM((1536, 128), F32),
            pltpu.VMEM((4096, 128), F32),
            pltpu.VMEM((4096, 128), F32),
            pltpu.VMEM((NB, 128, 128), BF16),
            pltpu.VMEM((128, NB * 128), BF16),
            pltpu.VMEM((RUNS, PLANES, RUN, 128), BF16),
            pltpu.VMEM((RUNS, PLANES, RUN, 128), BF16),
            pltpu.VMEM((1024, 128), F32),
            pltpu.VMEM((NB * KT + 8, 8, 128), F32),
            pltpu.VMEM((NB * KT, ALL_ROWS), BF16),
            pltpu.VMEM((512, NB * 128), BF16),
            pltpu.VMEM((PEERS, 8, ROWS, 128), BF16),
            pltpu.VMEM((PEERS, 8, ROWS, 128), BF16),
            pltpu.VMEM((PEERS, ROWS * 8, 128), BF16),
            pltpu.VMEM((PEERS, ROWS * 8, 128), BF16),
            pltpu.VMEM((2, ALL_ROWS, 512), BF16),
            pltpu.VMEM((ROWS * 8, 128), F32),
            pltpu.VMEM((RUNS, 2, RUN, 128), BF16),
            pltpu.VMEM((2, *tile), BF16),
            pltpu.VMEM((2, *tile), BF16),
            pltpu.VMEM((2, 2, *tile), BF16),
            pltpu.VMEM((2, 2, *tile), BF16),
            pltpu.VMEM((512, 128), F32),
            pltpu.VMEM((PLANES, *tile), F32),
            pltpu.VMEM((2, *tile), BF16),
            pltpu.VMEM((2, *tile), BF16),
            pltpu.VMEM((RAYS * NNZ, 128), jnp.int32),
            pltpu.SMEM((RAYS * NNZ, 128), jnp.int32),
            pltpu.VMEM((2 * NNZ, ALL_ROWS), F32),
            pltpu.SemaphoreType.DMA((7,)),
            pltpu.SemaphoreType.DMA((4,)),
            pltpu.SemaphoreType.DMA((PEERS,)),
            pltpu.SemaphoreType.DMA((PEERS,)),
            pltpu.SemaphoreType.DMA((PEERS,)),
            pltpu.SemaphoreType.DMA((PEERS,)),
            pltpu.SemaphoreType.DMA((RUNS + 5,)),
            pltpu.SemaphoreType.DMA((RUNS + 5,)),
        ],
        compiler_params=pltpu.CompilerParams(
            collective_id=0, has_side_effects=True, vmem_limit_bytes=60 * 1024 * 1024
        ),
    )(
        *lists, tile_count.T,
        to_rows(volume), to_rows(tv_split), to_rows(tv_dual),
        measured.reshape(4096, 128), fit_dual.reshape(4096, 128), footprints,
    )
    volume_next, split_next, tv_dual_next, fit_dual_next = pl.pallas_call(
        hand_on,
        out_shape=result,
        in_specs=[hbm] * 4,
        out_specs=[hbm] * 4,
        scratch_shapes=[
            *(pltpu.VMEM(leaf.shape, F32) for leaf in result),
            pltpu.SemaphoreType.DMA((8,)),
        ],
    )(*held)
    return (
        from_rows(volume_next, volume.shape),
        from_rows(split_next, tv_split.shape),
        from_rows(tv_dual_next, tv_dual.shape),
        fit_dual_next.reshape(fit_dual.shape),
    )


def solution(mesh):
    return jax.shard_map(
        shards,
        mesh=mesh,
        in_specs=(
            P(None, ("ang", "slab"), None),
            P(None, None, ("ang", "slab"), None),
            P(None, None, ("ang", "slab"), None),
            P("ang", None, None, None, "slab", None),
            P("ang", None, None, None, "slab", None),
            P(),
            P(),
            P(),
            P(),
        ),
        out_specs=(
            P(None, ("ang", "slab"), None),
            P(None, None, ("ang", "slab"), None),
            P(None, None, ("ang", "slab"), None),
            P("ang", None, None, None, "slab", None),
        ),
        check_vma=False,
    )
```

time: 69 us -> 54.6 us (0.79)
  local copies, waits for them, and re-layouts: 9.59 us -> 0 us
  Pallas kernels: 57.6 us -> 53.7 us
  other arithmetic: 0.78 us -> 0 us
    unnamed x7 -> x0, local copies, waits for them, and re-layouts: 7.41 us -> none
    pallas_call x1 -> x2, Pallas kernels: 57.6 us -> 53.7 us  [the longest x1 50 us: shards(): pl.pallas_call(kernel, out_shape=result, in_specs=[vmem] * 3 + [hbm] * 6,...]
    reshape x2 -> x0, local copies, waits for them, and re-layouts: 1.14 us -> none  [the longest x1 0.76 us: shards(): lax.dynamic_index_in_dim(code, half, 1, keepdims=False)]
    select_n x1 -> x0, other arithmetic: 0.78 us -> none  [shards(): code = jnp.where(live, code, DEAD).reshape(4, 2, 16, RAYS, NNZ)]
    another operation x1 -> x0, local copies, waits for them, and re-layouts: 0.75 us -> none  [shards(): code.reshape(-1)]
where the time goes in v1:
time: 54.6 us; the launch traced here: 54.4 us
  Pallas kernels  53.7 us (98%)
  between operations  0.64 us (1%)
    pallas_call x1, Pallas kernels, shards(): pl.pallas_call(kernel, out_shape=result, in_specs=[vmem] * 3 + [hbm] * 6,...  50 us
    pallas_call x1, Pallas kernels, shards(): pl.pallas_call(hand_on, out_shape=result, in_specs=[hbm] * 4, out_specs=[...  3.74 us

profile of v1, /device:TPU:1, one launch (start us, length us, event | category | flops | bytes accessed | tf_op | source)
XLA Modules:
  0.0 54.4 jit_solution(13656412849465295016)
XLA Ops:
  0.6 50.0 %shard_map.120 = (f32[512,128]{1,0:T(8,128)}, f32[1536,128]{1,0:T(8,128)}, f32[1536,128]{1,0:T(8,128)}, f32[4096,128]{1,0:T(8,128)}) custom-call(s32[64,128]{1,0:T(8,128)} %bitcast.45, s32[64,128]{1,0:T(8,128)} %bitcast.46, s32[8,128]{1,0:T(8,128)} %bitcast.47, f32[512,128]{1,0:T(8,128)} %bitcast.44, f32[1536,128]{1,0:T(8,128)} %bitcast.42, ...), custom_call_target="tpu_custom_call" | custom-call | tf_op jit(solution)/shard_map/pallas_call | solution.py:472
  50.7 3.7 %shard_map.121 = (f32[512,128]{1,0:T(8,128)}, f32[1536,128]{1,0:T(8,128)}, f32[1536,128]{1,0:T(8,128)}, f32[4096,128]{1,0:T(8,128)}) custom-call(f32[512,128]{1,0:T(8,128)} %get-tuple-element.12.refs_0_, f32[1536,128]{1,0:T(8,128)} %get-tuple-element.13.refs_1_, f32[1536,128]{1,0:T(8,128)} %get-tuple-element.14.refs_2_, f32[4096,128]{1,0:T(8,128)} %get-tuple-element.15.refs_3_), custom_call_target="tpu_custom_call" | custom-call | tf_op jit(solution)/shard_map/pallas_call | solution.py:526

commit v2 on v1

--- a/solution.py
+++ b/solution.py
@@ -16,6 +16,7 @@
 PLANES = 4
 ALL_ROWS = PEERS * ROWS
 DEAD = NB * KT
+WORDS = NB // 8
 RUNS = 4
 RUN = KT // RUNS
 TALL = 8
@@ -31,13 +32,13 @@
 
 def kernel(
     tile_ref, pick_ref, live_ref, vol_hbm, split_hbm, tvd_hbm, meas_hbm, dual_hbm, foot_hbm,
-    vol_out, split_out, tvd_out, fit_out,
-    vol_v, split_v, tvd_v, meas_v, dual_v, foot_v,
+    vol_v, split_v, tvd_v, dual_v,
+    meas_v, foot_v,
     foot_wide, vol_send, vol_recv, vol_rows, bank, counts, grouped,
     meas_send, meas_recv, proj_send, proj_recv, resid, ray_rows,
     first_recv, last_send, last_recv, part_send, part_recv, back_own, adj_v,
-    next_send, next_recv, code_v, codes, lanes_v,
-    local_sem, out_sem, meas_ssem, meas_rsem, proj_ssem, proj_rsem, one_ssem, one_rsem,
+    next_send, next_recv, code_v, codes, lanes_v, units_v,
+    local_sem, meas_ssem, meas_rsem, proj_ssem, proj_rsem, one_ssem, one_rsem,
 ):
     ang = lax.axis_index("ang")
     slab = lax.axis_index("slab")
@@ -146,25 +147,6 @@
             send_sem=ssem.at[px * 8 + pw], recv_sem=rsem.at[px * 8 + pw],
             device_id=(ang_of(px, pw), slab), device_id_type=MESH,
         )
-
-    pl.semaphore_wait(barrier, PEERS + 2)
-
-    def remote(src, dst, slot, device):
-        return pltpu.make_async_remote_copy(
-            src_ref=src, dst_ref=dst, send_sem=one_ssem.at[slot], recv_sem=one_rsem.at[slot],
-            device_id=device, device_id_type=MESH,
-        )
-
-    vol_copies = [
-        remote(vol_send.at[run], vol_recv.at[run], run, other) for run in range(RUNS)
-    ]
-    for copy in vol_copies:
-        copy.start()
-
-    @pl.loop(1, PEERS)
-    def _(i):
-        px, pw = peer_of(i)
-        exchange(meas_send, meas_recv, meas_ssem, meas_rsem, px, pw).start()
 
     entry_at = lax.broadcasted_iota(jnp.int32, (NNZ, 128), 0)
     lane = lax.broadcasted_iota(jnp.int32, (128, ALL_ROWS), 1)
@@ -190,24 +172,85 @@
     for b in range(NB):
         foot_wide[:, b * 128:(b + 1) * 128] = foot_v[b]
 
+    row_at = lax.broadcasted_iota(jnp.int32, (KT, TILE_WIDTH), 0)
+    col_at = lax.broadcasted_iota(jnp.int32, (KT, TILE_WIDTH), 1)
+    inner_row = row_at < KT - 1
+    inner_col = col_at < TILE_WIDTH - 1
+
+    def along(image, axis):
+        step = pltpu.roll(image, 127, axis) - image
+        return jnp.where(inner_row if axis == 0 else inner_col, step, 0.0)
+
+    def spread(part, axis):
+        part = jnp.where(inner_row if axis == 0 else inner_col, part, 0.0)
+        return pltpu.roll(part, 1, axis) - part
+
+    def force(i, c, z):
+        return plane(tvd_v, i * 2 + c, z) / penalty_tv - plane(split_v, i * 2 + c, z)
+
+    local[2].wait()
+    local[3].wait()
+    for c in range(2):
+        images = [plane(vol_v, c, z) for z in range(2)]
+        middle = images[1] - images[0] + force(0, c, 0)
+        above = force(0, c, 1) - images[1]
+        last_send[c] = above.astype(BF16)
+        for z, slices in enumerate((-middle, middle - above * keep)):
+            total = slices
+            for axis in range(2):
+                total = total + spread(along(images[z], axis) + force(1 + axis, c, z), axis)
+            adj_v[z * 2 + c] = penalty_tv * total
+
+    local[5].wait()
+
+    @pl.loop(0, ROWS)
+    def _(row):
+        rows = pl.ds(pl.multiple_of(row * 256, 256), 256)
+        dual_v[rows, :] = 0.5 * (dual_v[rows, :] - meas_v[rows, :])
+
+    pl.semaphore_wait(barrier, PEERS + 2)
+
+    def remote(src, dst, slot, device):
+        return pltpu.make_async_remote_copy(
+            src_ref=src, dst_ref=dst, send_sem=one_ssem.at[slot], recv_sem=one_rsem.at[slot],
+            device_id=device, device_id_type=MESH,
+        )
+
+    vol_copies = [
+        remote(vol_send.at[run], vol_recv.at[run], run, other) for run in range(RUNS)
+    ]
+    for copy in vol_copies:
+        copy.start()
+
+    @pl.loop(1, PEERS)
+    def _(i):
+        px, pw = peer_of(i)
+        exchange(meas_send, meas_recv, meas_ssem, meas_rsem, px, pw).start()
+
+    kernels = lanes_v[NNZ:2 * NNZ, :].astype(jnp.int32)
+    unit = jnp.left_shift(1, (kernels & 7) * 4)
+    for word in range(WORDS):
+        units_v[word] = jnp.where(jnp.right_shift(kernels, 3) == word, unit, 0)
+
     @pl.loop(0, 32)
     def _(step):
         kc = step // 4
         lt = step % 4
         lanes = pl.ds(pl.multiple_of(lt * 128, 128), 128)
         tile = (lax.broadcasted_iota(jnp.int32, (16, 128), 0) + kc * 16).astype(F32)
-        picks = []
-        for j in range(NNZ):
-            held = jnp.broadcast_to(lanes_v[j:j + 1, lanes], (16, 128)) == tile
-            pick = jnp.broadcast_to(lanes_v[NNZ + j:NNZ + j + 1, lanes], (16, 128))
-            picks.append(jnp.where(held, pick, -1.0).astype(BF16))
-        one = jnp.ones((16, 128), BF16)
-        zero = jnp.zeros((16, 128), BF16)
-        for b in range(NB):
-            hits = [jnp.where(pick == jnp.asarray(b, BF16), one, zero) for pick in picks]
-            while len(hits) > 1:
-                hits = [hits[n] + hits[n + 1] for n in range(0, len(hits), 2)]
-            counts[pl.ds(pl.multiple_of(b * 128 + kc * 16, 16), 16), lanes] = hits[0]
+        here = [
+            jnp.broadcast_to(lanes_v[j:j + 1, lanes], (16, 128)) == tile for j in range(NNZ)
+        ]
+        for word in range(WORDS):
+            total = None
+            for j in range(NNZ):
+                add = jnp.broadcast_to(units_v[word, j:j + 1, lanes], (16, 128))
+                add = jnp.where(here[j], add, 0)
+                total = add if total is None else total + add
+            for n in range(8):
+                count = lax.shift_right_logical(total, jnp.int32(4 * n)) & 15
+                at = pl.multiple_of((word * 8 + n) * 128 + kc * 16, 16)
+                counts[pl.ds(at, 16), lanes] = count.astype(F32).astype(BF16)
 
     for run in range(RUNS):
         vol_copies[run].wait_recv()
@@ -229,11 +272,6 @@
     first_copy = remote(vol_send.at[:, pl.ds(0, 2)], first_recv, RUNS, down_id)
     first_copy.start()
 
-    local[2].wait()
-    local[3].wait()
-    for c in range(2):
-        term = plane(tvd_v, c, 1) / penalty_tv - plane(split_v, c, 1) - plane(vol_v, c, 1)
-        last_send[c] = term.astype(BF16)
     last_copy = remote(last_send, last_recv, RUNS + 1, up_id)
     last_copy.start()
 
@@ -315,51 +353,28 @@
         part_copies[z].start()
     back_own[...] = backward(0, slice(0, 4))
 
-    row_at = lax.broadcasted_iota(jnp.int32, (KT, TILE_WIDTH), 0)
-    col_at = lax.broadcasted_iota(jnp.int32, (KT, TILE_WIDTH), 1)
-    inner_row = row_at < KT - 1
-    inner_col = col_at < TILE_WIDTH - 1
-
-    def along(image, axis):
-        step = pltpu.roll(image, 127, axis) - image
-        return jnp.where(inner_row if axis == 0 else inner_col, step, 0.0)
-
-    def spread(part, axis):
-        part = jnp.where(inner_row if axis == 0 else inner_col, part, 0.0)
-        return pltpu.roll(part, 1, axis) - part
-
-    def force(i, c, z):
-        return plane(tvd_v, i * 2 + c, z) / penalty_tv - plane(split_v, i * 2 + c, z)
-
     first_copy.wait_recv()
     last_copy.wait_recv()
-    for c in range(2):
-        images = [plane(vol_v, c, z) for z in range(2)]
-        below = (last_recv[c].astype(F32) + images[0]) * keep_below
-        middle = images[1] - images[0] + force(0, c, 0)
-        above = (first_recv[:, c].reshape(KT, 128).astype(F32) - images[1] + force(0, c, 1)) * keep
-        for z, slices in enumerate((below - middle, middle - above)):
-            total = slices
-            for axis in range(2):
-                total = total + spread(along(images[z], axis) + force(1 + axis, c, z), axis)
-            adj_v[z * 2 + c] = penalty_tv * total
-
     for z in range(2):
         part_copies[z].wait_recv()
         for c in range(2):
             cz = z * 2 + c
-            descent = back_own[cz * 128:(cz + 1) * 128, :] + part_recv[z, c].astype(F32) + adj_v[cz]
-            image = plane(vol_v, c, z) - step_size * descent
+            image = plane(vol_v, c, z)
+            if z == 0:
+                slices = (last_recv[c].astype(F32) + image) * keep_below
+            else:
+                slices = first_recv[:, c].reshape(KT, 128).astype(F32) * -keep
+            descent = (
+                back_own[cz * 128:(cz + 1) * 128, :] + part_recv[z, c].astype(F32)
+                + (adj_v[cz] + penalty_tv * slices)
+            )
+            image = image - step_size * descent
             vol_v[pl.ds(c * 256 + z, KT, stride=2), :] = image
             if z == 0:
                 next_send[c] = image.astype(BF16)
         if z == 0:
             next_copy = remote(next_send, next_recv, RUNS + 4, down_id)
             next_copy.start()
-    vol_done = pltpu.make_async_copy(vol_v, vol_out, out_sem.at[0])
-    vol_done.start()
-
-    local[5].wait()
 
     @pl.loop(1, PEERS)
     def _(i):
@@ -389,10 +404,7 @@
                         proj = one_of([turned[(n - g) % 4] for n in range(4)])
                         at = (two * 2 + row) * 256 + c * 128 + block // 2 * 32 + block % 2 * 8
                         rows = pl.ds(pl.multiple_of(at + (half + part) % 2 * 16, 8), 8)
-                        dual_v[rows, :] = 0.5 * (proj + dual_v[rows, :] - meas_v[rows, :])
-
-    fit_done = pltpu.make_async_copy(dual_v, fit_out, out_sem.at[1])
-    fit_done.start()
+                        dual_v[rows, :] = dual_v[rows, :] + 0.5 * proj
 
     for z in range(2):
         if z == 1:
@@ -412,10 +424,6 @@
                 split = arg - jnp.clip(arg, -bound, bound)
                 split_v[rows, :] = split
                 tvd_v[rows, :] = dual + penalty_tv * (steps[i] - split)
-    split_done = pltpu.make_async_copy(split_v, split_out, out_sem.at[2])
-    split_done.start()
-    tvd_done = pltpu.make_async_copy(tvd_v, tvd_out, out_sem.at[3])
-    tvd_done.start()
 
     for copy in (*vol_copies, first_copy, last_copy, *part_copies, next_copy):
         copy.wait_send()
@@ -426,21 +434,12 @@
         exchange(meas_send, meas_recv, meas_ssem, meas_rsem, px, pw).wait_send()
         exchange(proj_send, proj_recv, proj_ssem, proj_rsem, px, pw).wait_send()
 
-    for copy in (vol_done, fit_done, split_done, tvd_done):
-        copy.wait()
-
 
 def hand_on(*refs):
-    given, out, held = refs[:4], refs[4:8], refs[8:12]
-    sems = refs[12]
-    fetches = [pltpu.make_async_copy(given[n], held[n], sems.at[n]) for n in range(4)]
-    stores = [pltpu.make_async_copy(held[n], out[n], sems.at[4 + n]) for n in range(4)]
-    for copy in fetches:
+    copies = [pltpu.make_async_copy(refs[n], refs[4 + n], refs[8].at[n]) for n in range(4)]
+    for copy in copies:
         copy.start()
-    for fetch, store in zip(fetches, stores):
-        fetch.wait()
-        store.start()
-    for copy in stores:
+    for copy in copies:
         copy.wait()
 
 
@@ -471,14 +470,10 @@
     ]
     held = pl.pallas_call(
         kernel,
-        out_shape=result,
+        out_shape=[pltpu.VMEM(leaf.shape, F32) for leaf in result],
         in_specs=[vmem] * 3 + [hbm] * 6,
-        out_specs=[hbm] * 4,
+        out_specs=[vmem] * 4,
         scratch_shapes=[
-            pltpu.VMEM((512, 128), F32),
-            pltpu.VMEM((1536, 128), F32),
-            pltpu.VMEM((1536, 128), F32),
-            pltpu.VMEM((4096, 128), F32),
             pltpu.VMEM((4096, 128), F32),
             pltpu.VMEM((NB, 128, 128), BF16),
             pltpu.VMEM((128, NB * 128), BF16),
@@ -506,8 +501,8 @@
             pltpu.VMEM((RAYS * NNZ, 128), jnp.int32),
             pltpu.SMEM((RAYS * NNZ, 128), jnp.int32),
             pltpu.VMEM((2 * NNZ, ALL_ROWS), F32),
+            pltpu.VMEM((WORDS, NNZ, ALL_ROWS), jnp.int32),
             pltpu.SemaphoreType.DMA((7,)),
-            pltpu.SemaphoreType.DMA((4,)),
             pltpu.SemaphoreType.DMA((PEERS,)),
             pltpu.SemaphoreType.DMA((PEERS,)),
             pltpu.SemaphoreType.DMA((PEERS,)),
@@ -516,7 +511,7 @@
             pltpu.SemaphoreType.DMA((RUNS + 5,)),
         ],
         compiler_params=pltpu.CompilerParams(
-            collective_id=0, has_side_effects=True, vmem_limit_bytes=60 * 1024 * 1024
+            collective_id=0, has_side_effects=True, vmem_limit_bytes=52 * 1024 * 1024
         ),
     )(
         *lists, tile_count.T,
@@ -526,12 +521,10 @@
     volume_next, split_next, tv_dual_next, fit_dual_next = pl.pallas_call(
         hand_on,
         out_shape=result,
-        in_specs=[hbm] * 4,
+        in_specs=[vmem] * 4,
         out_specs=[hbm] * 4,
-        scratch_shapes=[
-            *(pltpu.VMEM(leaf.shape, F32) for leaf in result),
-            pltpu.SemaphoreType.DMA((8,)),
-        ],
+        scratch_shapes=[pltpu.SemaphoreType.DMA((4,))],
+        compiler_params=pltpu.CompilerParams(vmem_limit_bytes=2 * 1024 * 1024),
     )(*held)
     return (
         from_rows(volume_next, volume.shape),

time: 54.6 us -> 50.2 us (0.919)
  Pallas kernels: 53.7 us -> 49.4 us
    pallas_call x2, Pallas kernels: 53.7 us -> 49.4 us  [the longest x1 47.5 us: shards(): pl.pallas_call(kernel, out_shape=[pltpu.VMEM(leaf.shape, F32) for leaf in...]
where the time goes in v2:
time: 50.2 us; the launch traced here: 50.1 us
  Pallas kernels  49.4 us (98%)
  between operations  0.64 us (1%)
    pallas_call x1, Pallas kernels, shards(): pl.pallas_call(kernel, out_shape=[pltpu.VMEM(leaf.shape, F32) for leaf in...  47.5 us
    pallas_call x1, Pallas kernels, shards(): pl.pallas_call(hand_on, out_shape=result, in_specs=[vmem] * 4, out_specs=...  1.96 us

profile of v2, /device:TPU:1, one launch (start us, length us, event | category | flops | bytes accessed | tf_op | source)
XLA Modules:
  0.0 50.1 jit_solution(13782338512696464487)
XLA Ops:
  0.6 47.5 %shard_map.120 = (f32[512,128]{1,0:T(8,128)S(1)}, f32[1536,128]{1,0:T(8,128)S(1)}, f32[1536,128]{1,0:T(8,128)S(1)}, f32[4096,128]{1,0:T(8,128)S(1)}) custom-call(s32[64,128]{1,0:T(8,128)} %bitcast.45, s32[64,128]{1,0:T(8,128)} %bitcast.46, s32[8,128]{1,0:T(8,128)} %bitcast.47, f32[512,128]{1,0:T(8,128)} %bitcast.44, f32[1536,128]{1,0:T(8,128)} %bitcast.42, ...), custom_call_target="tpu_custom_call" | custom-call | tf_op jit(solution)/shard_map/pallas_call | solution.py:471
  48.1 2.0 %shard_map.121 = (f32[512,128]{1,0:T(8,128)}, f32[1536,128]{1,0:T(8,128)}, f32[1536,128]{1,0:T(8,128)}, f32[4096,128]{1,0:T(8,128)}) custom-call(f32[512,128]{1,0:T(8,128)S(1)} %get-tuple-element.12.refs_0_, f32[1536,128]{1,0:T(8,128)S(1)} %get-tuple-element.13.refs_1_, f32[1536,128]{1,0:T(8,128)S(1)} %get-tuple-element.14.refs_2_, ...), custom_call_target="tpu_custom_call" | custom-call | tf_op jit(solution)/shard_map/pallas_call | solution.py:521

commit v3 on v2

--- a/solution.py
+++ b/solution.py
@@ -19,7 +19,7 @@
 WORDS = NB // 8
 RUNS = 4
 RUN = KT // RUNS
-TALL = 8
+TALL = 20
 
 penalty_tv = 0.5
 tv_weight = 0.3

time: 50.2 us -> 48.8 us (0.972)
  Pallas kernels: 49.4 us -> 48 us
    pallas_call x1, Pallas kernels: 47.5 us -> 46.1 us  [shards(): pl.pallas_call(kernel, out_shape=[pltpu.VMEM(leaf.shape, F32) for leaf in...]
where the time goes in v3:
time: 48.8 us; the launch traced here: 48.7 us
  Pallas kernels  48 us (98%)
  between operations  0.64 us (1%)
    pallas_call x1, Pallas kernels, shards(): pl.pallas_call(kernel, out_shape=[pltpu.VMEM(leaf.shape, F32) for leaf in...  46.1 us
    pallas_call x1, Pallas kernels, shards(): pl.pallas_call(hand_on, out_shape=result, in_specs=[vmem] * 4, out_specs=...  1.96 us

profile of v3, /device:TPU:1, one launch (start us, length us, event | category | flops | bytes accessed | tf_op | source)
XLA Modules:
  0.0 48.7 jit_solution(15306403374311946821)
XLA Ops:
  0.6 46.1 %shard_map.120 = (f32[512,128]{1,0:T(8,128)S(1)}, f32[1536,128]{1,0:T(8,128)S(1)}, f32[1536,128]{1,0:T(8,128)S(1)}, f32[4096,128]{1,0:T(8,128)S(1)}) custom-call(s32[64,128]{1,0:T(8,128)} %bitcast.45, s32[64,128]{1,0:T(8,128)} %bitcast.46, s32[8,128]{1,0:T(8,128)} %bitcast.47, f32[512,128]{1,0:T(8,128)} %bitcast.44, f32[1536,128]{1,0:T(8,128)} %bitcast.42, ...), custom_call_target="tpu_custom_call" | custom-call | tf_op jit(solution)/shard_map/pallas_call | solution.py:471
  46.7 2.0 %shard_map.121 = (f32[512,128]{1,0:T(8,128)}, f32[1536,128]{1,0:T(8,128)}, f32[1536,128]{1,0:T(8,128)}, f32[4096,128]{1,0:T(8,128)}) custom-call(f32[512,128]{1,0:T(8,128)S(1)} %get-tuple-element.12.refs_0_, f32[1536,128]{1,0:T(8,128)S(1)} %get-tuple-element.13.refs_1_, f32[1536,128]{1,0:T(8,128)S(1)} %get-tuple-element.14.refs_2_, ...), custom_call_target="tpu_custom_call" | custom-call | tf_op jit(solution)/shard_map/pallas_call | solution.py:521
